TPU v7x, 256 devices: a whole 4x4x8 slice. The times are simulated.
256 devices in a mesh: seq: 16 (over x, y), head: 16 (over z, core).
Axes of the slice: x: 4, y: 4, z: 8, core: 2. Of those that a mesh axis runs over, the one named last changes fastest.
Arguments:
- activations: bfloat16 [65536, 768], P(('seq', 'head')), may hold values from -6 to 6
- ln_gain: bfloat16 [768], replicated, may hold values from 0.099609375 to 1.8984375
- w_query: bfloat16 [768, 768], replicated
- w_key: bfloat16 [768, 768], replicated
- w_value: bfloat16 [768, 768], replicated, may hold values from -0.21875 to 0.21875
- w_gate: bfloat16 [768, 768], replicated, may hold values from -0.21875 to 0.21875
- w_out: bfloat16 [768, 768], replicated, may hold values from -0.21875 to 0.21875
- bias_tiles: bfloat16 [16, 16, 128, 256], P(None, 'head'), may hold values from -6 to 6
- crop_lengths: int32 [16], replicated, may hold values from 1 to 16384, 65536 in all
- tile_index: int32 [512], P('seq'), may hold values from 0 to 15
- d_out: bfloat16 [65536, 768], P(('seq', 'head')), may hold values from -6 to 6
Outputs:
- d_activations: bfloat16 [65536, 768], P(('seq', 'head'))
- d_bias: float32 [16, 16, 128, 256], P(None, 'head')
Inputs may be any that keep to these rules, and one draw needn't show every extreme that they name: crop_lengths sum to 65536; the longest crop is exactly 16384 rows.
All inputs are finite; a program needn't handle non-finite values.
Results may differ from a plain program's by a relative error of at most 0.039.
The roundings to bfloat16 on the way count: a program that leaves them out, or rounds other values in their place, can miss the bound.
Values may be sent and summed in bfloat16 or wider, within the bound.
A program may use at most 128 MiB of HBM per device.

v0:
```python
import math
import jax
import jax.numpy as jnp
from jax import lax
from jax.sharding import PartitionSpec as P

BLOCK = 128
eps = 1e-05


def passed_along(array, axis, by):
    length = lax.axis_size(axis)
    pairs = [(i, i + by) for i in range(length) if 0 <= i + by < length]
    return lax.ppermute(array, axis, pairs)


def norm_rows(activations, ln_gain):
    values = activations.astype(jnp.float32)
    centred = values - jnp.mean(values, axis=1, keepdims=True)
    inverse = lax.rsqrt(jnp.mean(centred * centred, axis=1, keepdims=True) + eps)
    scaled = centred * inverse
    normed = (scaled * ln_gain.astype(jnp.float32)[None, :]).astype(jnp.bfloat16)
    return (normed, scaled, inverse)


def norm_back(d_normed, scaled, inverse, ln_gain):
    d_scaled = d_normed * ln_gain.astype(jnp.float32)[None, :]
    centre = jnp.mean(d_scaled, axis=1, keepdims=True)
    along = jnp.mean(d_scaled * scaled, axis=1, keepdims=True)
    return (inverse * (d_scaled - centre - scaled * along)).astype(jnp.bfloat16)


def window_mask(first, blocks, crop_lengths):
    bounds = jnp.cumsum(crop_lengths)

    def crop_of(positions):
        return jnp.sum((bounds[None, :] <= positions[:, None]).astype(jnp.int32), axis=1)

    queries = first + jnp.arange(blocks * BLOCK, dtype=jnp.int32)
    starts = first + BLOCK * jnp.arange(blocks, dtype=jnp.int32) - BLOCK
    key_pos = starts[:, None] + jnp.arange(2 * BLOCK, dtype=jnp.int32)[None, :]
    query_crop = crop_of(queries).reshape(blocks, BLOCK)
    key_crop = crop_of(key_pos.reshape(-1)).reshape(blocks, 2 * BLOCK)
    return (key_pos >= 0)[:, None, :] & (query_crop[:, :, None] == key_crop[:, None, :])


def attention_pass(
    queries, keys, values, keys_before, values_before, grad_out, bias, allowed, heads_here
):
    rows, width = queries.shape
    blocks = rows // BLOCK
    size = width // heads_here
    scale = 1.0 / math.sqrt(size)

    def split(array):
        return array.reshape(blocks, BLOCK, heads_here, size)

    query_blocks = split(queries)
    key_blocks = split(keys)
    value_blocks = split(values)
    grad_blocks = split(grad_out)
    key_prev = jnp.concatenate(
        [keys_before.reshape(1, BLOCK, heads_here, size), key_blocks[:-1]], axis=0
    )
    value_prev = jnp.concatenate(
        [values_before.reshape(1, BLOCK, heads_here, size), value_blocks[:-1]], axis=0
    )
    key_window = jnp.concatenate([key_prev, key_blocks], axis=1)
    value_window = jnp.concatenate([value_prev, value_blocks], axis=1)
    mask = allowed[:, None, :, :]
    scores = (
        jnp.einsum("nihd,njhd->nhij", query_blocks, key_window, preferred_element_type=jnp.float32)
        * scale
        + bias
    )
    scores = jnp.where(mask, scores, -1e30)
    top = jnp.max(scores, axis=3, keepdims=True)
    weights = jnp.where(mask, jnp.exp(scores - top), 0.0)
    probs = weights / jnp.sum(weights, axis=3, keepdims=True)
    probs_low = probs.astype(jnp.bfloat16)
    attended = jnp.einsum(
        "nhij,njhd->nihd", probs_low, value_window, preferred_element_type=jnp.float32
    )
    attended = attended.astype(jnp.bfloat16).reshape(rows, width)
    d_probs = jnp.einsum(
        "nihd,njhd->nhij", grad_blocks, value_window, preferred_element_type=jnp.float32
    )
    d_scores = probs * (d_probs - jnp.sum(probs * d_probs, axis=3, keepdims=True))
    d_low = d_scores.astype(jnp.bfloat16)
    d_queries = (
        jnp.einsum("nhij,njhd->nihd", d_low, key_window, preferred_element_type=jnp.float32) * scale
    )
    d_queries = d_queries.astype(jnp.bfloat16).reshape(rows, width)
    d_key_window = (
        jnp.einsum("nhij,nihd->njhd", d_low, query_blocks, preferred_element_type=jnp.float32)
        * scale
    )
    d_value_window = jnp.einsum(
        "nhij,nihd->njhd", probs_low, grad_blocks, preferred_element_type=jnp.float32
    )
    empty = jnp.zeros((1, BLOCK, heads_here, size), jnp.float32)
    d_keys = d_key_window[:, BLOCK:] + jnp.concatenate([d_key_window[1:, :BLOCK], empty], axis=0)
    d_values = d_value_window[:, BLOCK:] + jnp.concatenate(
        [d_value_window[1:, :BLOCK], empty], axis=0
    )
    return (
        attended,
        d_queries,
        d_keys.reshape(rows, width),
        d_values.reshape(rows, width),
        d_key_window[0, :BLOCK].reshape(BLOCK, width),
        d_value_window[0, :BLOCK].reshape(BLOCK, width),
        d_scores,
    )


def back_product(gradient, weight):
    return lax.dot_general(
        gradient, weight, (((1,), (1,)), ((), ())), preferred_element_type=jnp.float32
    )


def shards(
    activations,
    ln_gain,
    w_query,
    w_key,
    w_value,
    w_gate,
    w_out,
    bias_tiles,
    crop_lengths,
    tile_index,
    d_out,
):
    heads_here = bias_tiles.shape[1]
    normed, scaled, inverse = norm_rows(activations, ln_gain)
    queries = jnp.dot(normed, w_query, preferred_element_type=jnp.float32).astype(jnp.bfloat16)
    keys = jnp.dot(normed, w_key, preferred_element_type=jnp.float32).astype(jnp.bfloat16)
    values = jnp.dot(normed, w_value, preferred_element_type=jnp.float32).astype(jnp.bfloat16)
    gate_input = jnp.dot(normed, w_gate, preferred_element_type=jnp.float32).astype(jnp.bfloat16)
    d_mixed = back_product(d_out, w_out).astype(jnp.bfloat16)
    head_q, head_k, head_v, head_gin, head_dmix = (
        lax.all_to_all(queries, "head", split_axis=1, concat_axis=0, tiled=True),
        lax.all_to_all(keys, "head", split_axis=1, concat_axis=0, tiled=True),
        lax.all_to_all(values, "head", split_axis=1, concat_axis=0, tiled=True),
        lax.all_to_all(gate_input, "head", split_axis=1, concat_axis=0, tiled=True),
        lax.all_to_all(d_mixed, "head", split_axis=1, concat_axis=0, tiled=True),
    )
    head_gate = jax.nn.sigmoid(head_gin.astype(jnp.float32))
    head_grad = (head_dmix.astype(jnp.float32) * head_gate).astype(jnp.bfloat16)
    group_rows = head_q.shape[0]
    blocks = group_rows // BLOCK
    first = lax.axis_index("seq") * group_rows
    allowed = window_mask(first, blocks, crop_lengths)
    picks = (
        tile_index[:, None] == jnp.arange(bias_tiles.shape[0], dtype=jnp.int32)[None, :]
    ).astype(jnp.bfloat16)
    bias = jnp.einsum("nt,thij->nhij", picks, bias_tiles, preferred_element_type=jnp.float32)
    keys_before, values_before = passed_along((head_k[-BLOCK:], head_v[-BLOCK:]), "seq", 1)
    attended, d_queries, d_keys, d_values, d_key_edge, d_value_edge, d_scores = attention_pass(
        head_q, head_k, head_v, keys_before, values_before, head_grad, bias, allowed, heads_here
    )
    key_after, value_after = (
        passed_along(d_key_edge.astype(jnp.bfloat16), "seq", -1).astype(d_key_edge.dtype),
        passed_along(d_value_edge.astype(jnp.bfloat16), "seq", -1).astype(d_value_edge.dtype),
    )
    d_keys = jnp.concatenate([d_keys[:-BLOCK], d_keys[-BLOCK:] + key_after], axis=0).astype(
        jnp.bfloat16
    )
    d_values = jnp.concatenate([d_values[:-BLOCK], d_values[-BLOCK:] + value_after], axis=0).astype(
        jnp.bfloat16
    )
    local_tiles = jnp.einsum(
        "nt,nhij->thij", picks.astype(jnp.float32), d_scores, precision=lax.Precision.HIGHEST
    )
    d_bias = lax.psum(local_tiles.astype(jnp.bfloat16), "seq").astype(jnp.float32)
    head_dgate = (
        head_dmix.astype(jnp.float32) * attended.astype(jnp.float32) * head_gate * (1.0 - head_gate)
    ).astype(jnp.bfloat16)
    row_dq, row_dk, row_dv, d_gate = (
        lax.all_to_all(d_queries, "head", split_axis=0, concat_axis=1, tiled=True),
        lax.all_to_all(d_keys, "head", split_axis=0, concat_axis=1, tiled=True),
        lax.all_to_all(d_values, "head", split_axis=0, concat_axis=1, tiled=True),
        lax.all_to_all(head_dgate, "head", split_axis=0, concat_axis=1, tiled=True),
    )
    d_normed = back_product(row_dq, w_query)
    d_normed = d_normed + back_product(row_dk, w_key)
    d_normed = d_normed + back_product(row_dv, w_value)
    d_normed = d_normed + back_product(d_gate, w_gate)
    d_activations = norm_back(d_normed, scaled, inverse, ln_gain)
    return (d_activations, d_bias)


def solution(mesh):
    return jax.shard_map(
        shards,
        mesh=mesh,
        in_specs=(
            P(("seq", "head"), None),
            P(),
            P(),
            P(),
            P(),
            P(),
            P(),
            P(None, "head", None, None),
            P(),
            P("seq"),
            P(("seq", "head"), None),
        ),
        out_specs=(P(("seq", "head"), None), P(None, "head", None, None)),
        check_vma=False,
    )
```

profile of v0, /device:TPU:32, one launch (start us, length us, event | category | flops | bytes accessed | tf_op | source)
XLA Modules:
  0.0 312.4 jit_solution(1983866665688578780)
XLA Ops:
  7.2 1.2 convert_reduce_fusion
  8.4 1.2 fusion.33
  10.4 1.9 convolution_convert_fusion.4
  12.4 0.9 copy.104
  13.3 8.6 %all-to-all-start.1 = ((bf16[256,16,48]{0,2,1:T(8,128)(2,1)}), bf16[256,16,48]{0,2,1:T(8,128)(2,1)S(1)}, u32[]{:S(2)}, u32[]{:S(2)}) async-start(bf16[256,16,48]{0,2,1:T(8,128)(2,1)} %bitcast.6), calls=%async_computation.1 | async-start | bytes 786432 | tf_op jit(solution)/shard_map/all_to_all | solution.py:144
  22.4 0.9 copy.110
  23.3 10.4 %all-to-all-done.1 = bf16[256,16,48]{0,2,1:T(8,128)(2,1)S(1)} async-done(((bf16[256,16,48]{0,2,1:T(8,128)(2,1)}), bf16[256,16,48]{0,2,1:T(8,128)(2,1)S(1)}, u32[]{:S(2)}, u32[]{:S(2)}) %all-to-all-start.1) | async-done | bytes 393248 | tf_op jit(solution)/shard_map/all_to_all | solution.py:144
  33.8 5.5 %all-to-all-start.3 = ((bf16[256,16,48]{0,2,1:T(8,128)(2,1)}), bf16[256,16,48]{0,2,1:T(8,128)(2,1)S(1)}, u32[]{:S(2)}, u32[]{:S(2)}) async-start(bf16[256,16,48]{0,2,1:T(8,128)(2,1)} %bitcast.11), calls=%async_computation.3 | async-start | bytes 786432 | tf_op jit(solution)/shard_map/all_to_all | solution.py:147
  39.3 1.3 convolution_convert_fusion.1
  40.6 1.9 copy.112
  42.5 8.9 %all-to-all-done.3 = bf16[256,16,48]{0,2,1:T(8,128)(2,1)S(1)} async-done(((bf16[256,16,48]{0,2,1:T(8,128)(2,1)}), bf16[256,16,48]{0,2,1:T(8,128)(2,1)S(1)}, u32[]{:S(2)}, u32[]{:S(2)}) %all-to-all-start.3) | async-done | bytes 393248 | tf_op jit(solution)/shard_map/all_to_all | solution.py:147
  51.4 5.3 %all-to-all-start.4 = ((bf16[256,16,48]{0,2,1:T(8,128)(2,1)}), bf16[256,16,48]{0,2,1:T(8,128)(2,1)S(1)}, u32[]{:S(2)}, u32[]{:S(2)}) async-start(bf16[256,16,48]{0,2,1:T(8,128)(2,1)} %bitcast.13), calls=%async_computation.4 | async-start | bytes 786432 | tf_op jit(solution)/shard_map/all_to_all | solution.py:146
  56.7 1.8 convolution_convert_fusion.5
  58.5 0.9 copy.98
  59.5 9.4 %all-to-all-done.4 = bf16[256,16,48]{0,2,1:T(8,128)(2,1)S(1)} async-done(((bf16[256,16,48]{0,2,1:T(8,128)(2,1)}), bf16[256,16,48]{0,2,1:T(8,128)(2,1)S(1)}, u32[]{:S(2)}, u32[]{:S(2)}) %all-to-all-start.4) | async-done | bytes 393248 | tf_op jit(solution)/shard_map/all_to_all | solution.py:146
  68.8 5.3 %all-to-all-start = ((bf16[256,16,48]{0,2,1:T(8,128)(2,1)}), bf16[256,16,48]{0,2,1:T(8,128)(2,1)S(1)}, u32[]{:S(2)}, u32[]{:S(2)}) async-start(bf16[256,16,48]{0,2,1:T(8,128)(2,1)} %bitcast), calls=%async_computation | async-start | bytes 786432 | tf_op jit(solution)/shard_map/all_to_all | solution.py:145
  75.5 1.9 convolution_convert_fusion.3
  77.4 0.9 copy.109
  78.4 1.5 convert_reduce_fusion.1
  79.9 6.3 %all-to-all-done = bf16[256,16,48]{0,2,1:T(8,128)(2,1)S(1)} async-done(((bf16[256,16,48]{0,2,1:T(8,128)(2,1)}), bf16[256,16,48]{0,2,1:T(8,128)(2,1)S(1)}, u32[]{:S(2)}, u32[]{:S(2)}) %all-to-all-start) | async-done | bytes 393248 | tf_op jit(solution)/shard_map/all_to_all | solution.py:145
  86.2 5.3 %all-to-all-start.2 = ((bf16[256,16,48]{0,2,1:T(8,128)(2,1)}), bf16[256,16,48]{0,2,1:T(8,128)(2,1)S(1)}, u32[]{:S(2)}, u32[]{:S(2)}) async-start(bf16[256,16,48]{0,2,1:T(8,128)(2,1)} %bitcast.168), calls=%async_computation.2 | async-start | bytes 786432 | tf_op jit(solution)/shard_map/all_to_all | solution.py:148
  91.5 1.4 eq.32
  92.9 1.4 convert_reduce_fusion.2
  94.3 1.3 fusion.46
  95.5 4.1 %fusion.16 = f32[32,128,256]{2,0,1:T(8,128)} fusion(bf16[16,128,256]{2,1,0:T(8,128)(2,1)} %bitcast.180, s32[32]{0:T(128)} %param.20), kind=kOutput, calls=%fused_computation.29 | convolution fusion | flops 33554944 | bytes 5243008 | tf_op jit(solution)/shard_map/nt,thij->nhij/dot_general | solution.py:159
  100.5 1.1 reshape.250
  101.6 0.9 copy.113
  102.5 1.9 reshape.253
  104.3 1.1 copy.115
  107.0 4.1 %collective-permute-start.1 = (bf16[128,48]{0,1:T(8,128)(2,1)}, bf16[128,48]{0,1:T(8,128)(2,1)}, u32[]{:S(2)}, u32[]{:S(2)}) collective-permute-start(bf16[128,48]{0,1:T(8,128)(2,1)} %slice.78), channel_id=1, source_target_pairs={{0,16},{16,32},{32,48},{48,64},{64,80},{80,96},{96,112},{112,128},... | collective-permute-start | bytes 36872 | tf_op jit(solution)/shard_map/ppermute | solution.py:14
  111.1 3.5 %collective-permute-start = (bf16[128,48]{0,1:T(8,128)(2,1)S(1)}, bf16[128,48]{0,1:T(8,128)(2,1)}, u32[]{:S(2)}, u32[]{:S(2)}) collective-permute-start(bf16[128,48]{0,1:T(8,128)(2,1)S(1)} %slice.76), channel_id=1, source_target_pairs={{0,16},{16,32},{32,48},{48,64},{64,80},{80,96},{96,112},{112,128},... | collective-permute-start | bytes 36872 | tf_op jit(solution)/shard_map/ppermute | solution.py:14
  114.6 1.0 fusion.39
  115.7 0.9 reshape.246
  116.6 1.1 copy.101
  118.5 1.1 copy.111
  119.8 12.2 %fusion.67 = (f32[32,128]{1,0:T(8,128)S(1)}, f32[32,128,256]{2,1,0:T(8,128)}) fusion(s32[32,256]{1,0:T(8,128)} %eq.32, s32[32,128]{1,0:T(8,128)} %bitcast.184, pred[32,256]{1,0:T(8,128)(4,1)} %fusion.46, f32[32,128,256]{2,0,1:T(8,128)} %fusion.16, bf16[32,128,48]{1,0,2:T(8,128)(2,1)S(1)} %reshape.250, bf16[32,128,1,48]{1,3,0,2:T(8,128)(2,1)S(1)} %copy.101, ...), kind=kOutput, calls=%fused_computation.106 | convolution fusion | flops 113508608 | bytes 9641984 | tf_op jit(solution)/shard_map/sub | solution.py:78
  132.0 3.0 fusion.19
  135.6 2.6 multiply_reduce_fusion
  138.2 1.4 subtract_multiply_fusion
  139.7 1.6 fusion.12
  142.8 1.3 collective-permute-start.3
  144.1 1.0 slice_add_fusion
  146.0 1.9 all_to_all.125
  147.9 1.9 copy.119
  149.7 7.2 %all-to-all-start.5 = ((bf16[16,256,48]{1,2,0:T(8,128)(2,1)}), bf16[16,256,48]{1,2,0:T(8,128)(2,1)}, u32[]{:S(2)}, u32[]{:S(2)}) async-start(bf16[16,256,48]{1,2,0:T(8,128)(2,1)} %copy.119), calls=%async_computation.5 | async-start | bytes 786432 | tf_op jit(solution)/shard_map/all_to_all | solution.py:182
  157.6 1.2 slice.110
  159.0 1.3 collective-permute-start.2
  160.3 1.0 slice.81
  162.9 6.1 %all-to-all-done.5 = bf16[16,256,48]{1,2,0:T(8,128)(2,1)} async-done(((bf16[16,256,48]{1,2,0:T(8,128)(2,1)}), bf16[16,256,48]{1,2,0:T(8,128)(2,1)}, u32[]{:S(2)}, u32[]{:S(2)}) %all-to-all-start.5) | async-done | bytes 393248 | tf_op jit(solution)/shard_map/all_to_all | solution.py:182
  169.0 5.8 %all-to-all-start.7 = ((bf16[16,256,48]{1,2,0:T(8,128)(2,1)}), bf16[16,256,48]{1,2,0:T(8,128)(2,1)}, u32[]{:S(2)}, u32[]{:S(2)}) async-start(bf16[16,256,48]{1,2,0:T(8,128)(2,1)} %bitcast.169), calls=%async_computation.7 | async-start | bytes 786432 | tf_op jit(solution)/shard_map/all_to_all | solution.py:184
  174.8 1.2 slice_add_fusion.1
  177.9 9.1 %all-to-all-done.7 = bf16[16,256,48]{1,2,0:T(8,128)(2,1)} async-done(((bf16[16,256,48]{1,2,0:T(8,128)(2,1)}), bf16[16,256,48]{1,2,0:T(8,128)(2,1)}, u32[]{:S(2)}, u32[]{:S(2)}) %all-to-all-start.7) | async-done | bytes 393248 | tf_op jit(solution)/shard_map/all_to_all | solution.py:184
  187.0 5.7 %all-to-all-start.6 = ((bf16[16,256,48]{1,2,0:T(8,128)(2,1)}), bf16[16,256,48]{1,2,0:T(8,128)(2,1)}, u32[]{:S(2)}, u32[]{:S(2)}) async-start(bf16[16,256,48]{1,2,0:T(8,128)(2,1)} %bitcast.157), calls=%async_computation.6 | async-start | bytes 786432 | tf_op jit(solution)/shard_map/all_to_all | solution.py:183
  193.0 3.1 %fusion.15 = f32[32,128,1,48]{1,3,0,2:T(8,128)S(1)} fusion(bf16[32,128,1,48]{1,3,0,2:T(8,128)(2,1)S(1)} %copy-done.10, bf16[31,128,1,48]{1,3,0,2:T(8,128)(2,1)S(1)} %copy-done.16, bf16[1,128,1,48]{1,3,0,2:T(8,128)(2,1)} %bitcast.15, f32[32,128,256]{2,1,0:T(8,128)} %get-tuple-element.13, f32[32,128]{1,0:T(8,128)S(1)} %get-tuple-element.12), kind=kOutput, calls=%fused_computation.28 | convolution fusion | flops 105512960 | bytes 5783552 | tf_op jit(solution)/shard_map/nhij,njhd->nihd/dot_general | solution.py:81
  196.8 6.9 %fusion.7 = bf16[16,1,128,256]{3,0,2,1:T(8,128)(2,1)} fusion(f32[32,128,256]{2,1,0:T(8,128)} %copy-done.1, s32[32]{0:T(128)S(1)} %copy-done.25), kind=kOutput, calls=%fused_computation.12 | convolution fusion | flops 201851392 | bytes 5243008 | tf_op jit(solution)/shard_map/nt,nhij->thij/dot_general | solution.py:174
  203.7 1.3 fusion.38
  205.0 7.4 %all-to-all-start.8 = ((bf16[16,256,48]{1,2,0:T(8,128)(2,1)}), bf16[16,256,48]{1,2,0:T(8,128)(2,1)S(1)}, u32[]{:S(2)}, u32[]{:S(2)}) async-start(bf16[16,256,48]{1,2,0:T(8,128)(2,1)} %fusion.38), calls=%async_computation.8 | async-start | bytes 786432 | tf_op jit(solution)/shard_map/all_to_all | solution.py:185
  212.4 1.9 fusion.70
  214.4 1.6 convolution_add_fusion.2
  216.0 1.5 convolution_add_fusion.1
  217.5 6.8 %all-to-all-done.8 = bf16[16,256,48]{1,2,0:T(8,128)(2,1)S(1)} async-done(((bf16[16,256,48]{1,2,0:T(8,128)(2,1)}), bf16[16,256,48]{1,2,0:T(8,128)(2,1)S(1)}, u32[]{:S(2)}, u32[]{:S(2)}) %all-to-all-start.8) | async-done | bytes 393248 | tf_op jit(solution)/shard_map/all_to_all | solution.py:185
  225.0 1.0 fusion.32
  226.0 76.6 %all-reduce.4.cloned.1.call-done = bf16[16,1,128,256]{3,0,2,1:T(8,128)(2,1)} async-done(((bf16[16,1,128,256]{3,0,2,1:T(8,128)(2,1)}), bf16[16,1,128,256]{3,0,2,1:T(8,128)(2,1)}) %all-reduce.4.cloned.1.call-update) | async-done | bytes 1048592 | tf_op jit(solution)/shard_map/psum | solution.py:177
  302.7 2.9 copy.133
  (102 shorter events, 14.9 us)
Async XLA Ops:
  7.2 14.7 %copy-start = (bf16[768,768]{1,0:T(8,128)(2,1)S(1)}, bf16[768,768]{1,0:T(8,128)(2,1)}, u32[]{:S(2)}) copy-start(bf16[768,768]{1,0:T(8,128)(2,1)} %param.16) | copy-start | bytes 3538948
  8.4 48.3 %copy-start.17 = (f32[256]{0:T(256)}, f32[256]{0:T(256)S(1)}, u32[]{:S(2)}) copy-start(f32[256]{0:T(256)S(1)} %broadcast_multiply_fusion.2) | copy-start | bytes 3076
  9.7 12.2 %copy-start.2 = (bf16[256,768]{1,0:T(8,128)(2,1)S(1)}, bf16[256,768]{1,0:T(8,128)(2,1)}, u32[]{:S(2)}) copy-start(bf16[256,768]{1,0:T(8,128)(2,1)} %param.11) | copy-start | bytes 1179652
  9.7 47.0 %copy-start.21 = (f32[256]{0:T(256)}, f32[256]{0:T(256)S(1)}, u32[]{:S(2)}) copy-start(f32[256]{0:T(256)S(1)} %add_rsqrt_fusion) | copy-start | bytes 3076
  10.4 46.3 %copy-start.19 = (f32[768]{0:T(1024)}, f32[768]{0:T(1024)S(1)}, u32[]{:S(2)}) copy-start(f32[768]{0:T(1024)S(1)} %convert_element_type.142) | copy-start | bytes 9220
  13.3 20.5 %all-to-all-start.1 = ((bf16[256,16,48]{0,2,1:T(8,128)(2,1)}), bf16[256,16,48]{0,2,1:T(8,128)(2,1)S(1)}, u32[]{:S(2)}, u32[]{:S(2)}) async-start(bf16[256,16,48]{0,2,1:T(8,128)(2,1)} %bitcast.6), calls=%async_computation.1 | async-start | bytes 786432 | tf_op jit(solution)/shard_map/all_to_all | solution.py:144
  21.9 17.4 %copy-start.13 = (bf16[768,768]{1,0:T(8,128)(2,1)S(1)}, bf16[768,768]{1,0:T(8,128)(2,1)}, u32[]{:S(2)}) copy-start(bf16[768,768]{1,0:T(8,128)(2,1)} %param.15) | copy-start | bytes 3538948
  33.8 17.6 %all-to-all-start.3 = ((bf16[256,16,48]{0,2,1:T(8,128)(2,1)}), bf16[256,16,48]{0,2,1:T(8,128)(2,1)S(1)}, u32[]{:S(2)}, u32[]{:S(2)}) async-start(bf16[256,16,48]{0,2,1:T(8,128)(2,1)} %bitcast.11), calls=%async_computation.3 | async-start | bytes 786432 | tf_op jit(solution)/shard_map/all_to_all | solution.py:147
  51.4 17.4 %all-to-all-start.4 = ((bf16[256,16,48]{0,2,1:T(8,128)(2,1)}), bf16[256,16,48]{0,2,1:T(8,128)(2,1)S(1)}, u32[]{:S(2)}, u32[]{:S(2)}) async-start(bf16[256,16,48]{0,2,1:T(8,128)(2,1)} %bitcast.13), calls=%async_computation.4 | async-start | bytes 786432 | tf_op jit(solution)/shard_map/all_to_all | solution.py:146
  56.7 17.4 %copy-start.26 = (s32[16]{0:T(128)S(1)}, s32[16]{0:T(128)}, u32[]{:S(2)}) copy-start(s32[16]{0:T(128)} %param.19) | copy-start | bytes 196
  68.8 17.4 %all-to-all-start = ((bf16[256,16,48]{0,2,1:T(8,128)(2,1)}), bf16[256,16,48]{0,2,1:T(8,128)(2,1)S(1)}, u32[]{:S(2)}, u32[]{:S(2)}) async-start(bf16[256,16,48]{0,2,1:T(8,128)(2,1)} %bitcast), calls=%async_computation | async-start | bytes 786432 | tf_op jit(solution)/shard_map/all_to_all | solution.py:145
  74.4 11.9 %copy-start.23 = (s32[16]{0:T(128)}, s32[16]{0:T(128)S(1)}, u32[]{:S(2)}) copy-start(s32[16]{0:T(128)S(1)} %reduce.6) | copy-start | bytes 196
  74.4 0.5 copy-start.24
  86.2 28.3 %all-to-all-start.2 = ((bf16[256,16,48]{0,2,1:T(8,128)(2,1)}), bf16[256,16,48]{0,2,1:T(8,128)(2,1)S(1)}, u32[]{:S(2)}, u32[]{:S(2)}) async-start(bf16[256,16,48]{0,2,1:T(8,128)(2,1)} %bitcast.168), calls=%async_computation.2 | async-start | bytes 786432 | tf_op jit(solution)/shard_map/all_to_all | solution.py:148
  101.6 18.2 %copy-start.6 = (bf16[32,128,48]{1,0,2:T(8,128)(2,1)}, bf16[32,128,48]{1,0,2:T(8,128)(2,1)S(1)}, u32[]{:S(2)}) copy-start(bf16[32,128,48]{1,0,2:T(8,128)(2,1)S(1)} %reshape.250) | copy-start | bytes 1179652
  105.5 5.6 %copy-start.8 = (bf16[32,128,1,48]{1,3,0,2:T(8,128)(2,1)}, bf16[32,128,1,48]{1,3,0,2:T(8,128)(2,1)S(1)}, u32[]{:S(2)}) copy-start(bf16[32,128,1,48]{1,3,0,2:T(8,128)(2,1)S(1)} %copy.115) | copy-start | bytes 1179652
  107.0 28.1 %collective-permute-start.1 = (bf16[128,48]{0,1:T(8,128)(2,1)}, bf16[128,48]{0,1:T(8,128)(2,1)}, u32[]{:S(2)}, u32[]{:S(2)}) collective-permute-start(bf16[128,48]{0,1:T(8,128)(2,1)} %slice.78), channel_id=1, source_target_pairs={{0,16},{16,32},{32,48},{48,64},{64,80},{80,96},{96,112},{112,128},... | collective-permute-start | bytes 36872 | tf_op jit(solution)/shard_map/ppermute | solution.py:14
  111.1 8.7 %collective-permute-start = (bf16[128,48]{0,1:T(8,128)(2,1)S(1)}, bf16[128,48]{0,1:T(8,128)(2,1)}, u32[]{:S(2)}, u32[]{:S(2)}) collective-permute-start(bf16[128,48]{0,1:T(8,128)(2,1)S(1)} %slice.76), channel_id=1, source_target_pairs={{0,16},{16,32},{32,48},{48,64},{64,80},{80,96},{96,112},{112,128},... | collective-permute-start | bytes 36872 | tf_op jit(solution)/shard_map/ppermute | solution.py:14
  114.6 3.9 %copy-start.4 = (bf16[256,16,48]{0,2,1:T(8,128)(2,1)}, bf16[256,16,48]{0,2,1:T(8,128)(2,1)S(1)}, u32[]{:S(2)}) copy-start(bf16[256,16,48]{0,2,1:T(8,128)(2,1)S(1)} %all-to-all-done.2) | copy-start | bytes 1179652
  132.0 3.4 %copy-start.3 = (f32[32,128,256]{2,1,0:T(8,128)S(1)}, f32[32,128,256]{2,1,0:T(8,128)}, u32[]{:S(2)}) copy-start(f32[32,128,256]{2,1,0:T(8,128)} %get-tuple-element.13) | copy-start | bytes 12582916
  132.0 3.5 %copy-start.9 = (bf16[32,128,1,48]{1,3,0,2:T(8,128)(2,1)S(1)}, bf16[32,128,1,48]{1,3,0,2:T(8,128)(2,1)}, u32[]{:S(2)}) copy-start(bf16[32,128,1,48]{1,3,0,2:T(8,128)(2,1)} %copy-done.8) | copy-start | bytes 1179652
  132.0 3.6 %copy-start.15 = (bf16[31,128,1,48]{1,3,0,2:T(8,128)(2,1)S(1)}, bf16[31,128,1,48]{1,3,0,2:T(8,128)(2,1)}, u32[]{:S(2)}) copy-start(bf16[31,128,1,48]{1,3,0,2:T(8,128)(2,1)} %slice.79) | copy-start | bytes 1142788
  138.2 1.4 copy-start.11
  139.6 2.0 copy-start.1
  139.6 2.0 copy-start.7
  142.8 18.6 %collective-permute-start.3 = (bf16[128,48]{0,1:T(8,128)(2,1)}, bf16[128,48]{0,1:T(8,128)(2,1)}, u32[]{:S(2)}, u32[]{:S(2)}) collective-permute-start(bf16[128,48]{0,1:T(8,128)(2,1)} %fusion.52), channel_id=1, source_target_pairs={{16,0},{32,16},{48,32},{64,48},{80,64},{96,80},{112,96},{128,112},... | collective-permute-start | bytes 36872 | tf_op jit(solution)/shard_map/ppermute | solution.py:14
  149.7 19.2 %all-to-all-start.5 = ((bf16[16,256,48]{1,2,0:T(8,128)(2,1)}), bf16[16,256,48]{1,2,0:T(8,128)(2,1)}, u32[]{:S(2)}, u32[]{:S(2)}) async-start(bf16[16,256,48]{1,2,0:T(8,128)(2,1)} %copy.119), calls=%async_computation.5 | async-start | bytes 786432 | tf_op jit(solution)/shard_map/all_to_all | solution.py:182
  159.0 17.4 %collective-permute-start.2 = (bf16[128,48]{0,1:T(8,128)(2,1)}, bf16[128,48]{0,1:T(8,128)(2,1)}, u32[]{:S(2)}, u32[]{:S(2)}) collective-permute-start(bf16[128,48]{0,1:T(8,128)(2,1)} %fusion.51), channel_id=1, source_target_pairs={{16,0},{32,16},{48,32},{64,48},{80,64},{96,80},{112,96},{128,112},... | collective-permute-start | bytes 36872 | tf_op jit(solution)/shard_map/ppermute | solution.py:14
  169.0 18.1 %all-to-all-start.7 = ((bf16[16,256,48]{1,2,0:T(8,128)(2,1)}), bf16[16,256,48]{1,2,0:T(8,128)(2,1)}, u32[]{:S(2)}, u32[]{:S(2)}) async-start(bf16[16,256,48]{1,2,0:T(8,128)(2,1)} %bitcast.169), calls=%async_computation.7 | async-start | bytes 786432 | tf_op jit(solution)/shard_map/all_to_all | solution.py:184
  176.1 16.9 %copy-start.10 = (bf16[32,128,1,48]{1,3,0,2:T(8,128)(2,1)S(1)}, bf16[32,128,1,48]{1,3,0,2:T(8,128)(2,1)}, u32[]{:S(2)}) copy-start(bf16[32,128,1,48]{1,3,0,2:T(8,128)(2,1)} %copy-done.8) | copy-start | bytes 1179652
  176.1 16.9 %copy-start.16 = (bf16[31,128,1,48]{1,3,0,2:T(8,128)(2,1)S(1)}, bf16[31,128,1,48]{1,3,0,2:T(8,128)(2,1)}, u32[]{:S(2)}) copy-start(bf16[31,128,1,48]{1,3,0,2:T(8,128)(2,1)} %slice.79) | copy-start | bytes 1142788
  187.0 18.0 %all-to-all-start.6 = ((bf16[16,256,48]{1,2,0:T(8,128)(2,1)}), bf16[16,256,48]{1,2,0:T(8,128)(2,1)}, u32[]{:S(2)}, u32[]{:S(2)}) async-start(bf16[16,256,48]{1,2,0:T(8,128)(2,1)} %bitcast.157), calls=%async_computation.6 | async-start | bytes 786432 | tf_op jit(solution)/shard_map/all_to_all | solution.py:183
  192.7 110.0 %all-reduce.4.cloned.1.call-start = ((), (), s32[]{:S(2)}) async-start(), calls=%async_computation.9 | async-start | bytes 2097152 | tf_op jit(solution)/shard_map/psum | solution.py:177
  196.1 0.7 copy-start.25
  196.8 6.9 %copy-start.5 = (bf16[256,16,48]{0,2,1:T(8,128)(2,1)S(1)}, bf16[256,16,48]{0,2,1:T(8,128)(2,1)}, u32[]{:S(2)}) copy-start(bf16[256,16,48]{0,2,1:T(8,128)(2,1)} %copy-done.4) | copy-start | bytes 1179652
  205.0 9.3 %copy-start.12 = (bf16[768,768]{1,0:T(8,128)(2,1)S(1)}, bf16[768,768]{1,0:T(8,128)(2,1)}, u32[]{:S(2)}) copy-start(bf16[768,768]{1,0:T(8,128)(2,1)} %param.14) | copy-start | bytes 3538948
  205.0 19.3 %all-to-all-start.8 = ((bf16[16,256,48]{1,2,0:T(8,128)(2,1)}), bf16[16,256,48]{1,2,0:T(8,128)(2,1)S(1)}, u32[]{:S(2)}, u32[]{:S(2)}) async-start(bf16[16,256,48]{1,2,0:T(8,128)(2,1)} %fusion.38), calls=%async_computation.8 | async-start | bytes 786432 | tf_op jit(solution)/shard_map/all_to_all | solution.py:185
  214.3 1.7 copy-start.14
  216.0 8.3 %copy-start.18 = (f32[256]{0:T(256)S(1)}, f32[256]{0:T(256)}, u32[]{:S(2)}) copy-start(f32[256]{0:T(256)} %copy-done.17) | copy-start | bytes 3076
  216.0 8.3 %copy-start.20 = (f32[768]{0:T(1024)S(1)}, f32[768]{0:T(1024)}, u32[]{:S(2)}) copy-start(f32[768]{0:T(1024)} %copy-done.19) | copy-start | bytes 9220
  216.0 8.3 %copy-start.22 = (f32[256]{0:T(256)S(1)}, f32[256]{0:T(256)}, u32[]{:S(2)}) copy-start(f32[256]{0:T(256)} %copy-done.21) | copy-start | bytes 3076
Sparse Core Ops, SparseCore 0:
  203.8 98.8 all-reduce.3
where the time goes:
time: 315 us; the launch traced here: 312 us
  waiting for transfers between devices  134 us (43%)
  starting transfers between devices  66.5 us (21%)
  matrix products  47.2 us (15%)
  local copies, waits for them, and re-layouts  34.3 us (11%)
  other arithmetic  16.1 us (5%)
  between operations  14.6 us (5%)
    psum x1, waiting for transfers between devices, shards(): lax.psum(local_tiles.astype(jnp.bfloat16), 'seq').astype(jnp.float32)  76.6 us
    sub x1, matrix products, attention_pass(): weights = jnp.where(mask, jnp.exp(scores - top), 0.0)  12.2 us
    all_to_all x1, waiting for transfers between devices, shards(): lax.all_to_all(queries, 'head', split_axis=1, concat_axis=0, tiled=True)  10.4 us
    ppermute x4, starting transfers between devices, passed_along(): return lax.ppermute(array, axis, pairs)  10.1 us
    all_to_all x1, waiting for transfers between devices, shards(): lax.all_to_all(values, 'head', split_axis=1, concat_axis=0, tiled=True)  9.37 us
    all_to_all x1, waiting for transfers between devices, shards(): lax.all_to_all(d_values, 'head', split_axis=0, concat_axis=1, tiled=True)  9.12 us
    all_to_all x1, waiting for transfers between devices, shards(): lax.all_to_all(gate_input, 'head', split_axis=1, concat_axis=0, tiled=True)  8.9 us
    all_to_all x1, starting transfers between devices, shards(): lax.all_to_all(queries, 'head', split_axis=1, concat_axis=0, tiled=True)  8.59 us
  transfers between devices with their start and end apart: 14, of which 8 were waited for; matrix products, arithmetic and copies ran while one was open for 25% of the time, Pallas kernels for 0%

commit v1 on v0

--- a/solution.py
+++ b/solution.py
@@ -174,7 +174,9 @@
     local_tiles = jnp.einsum(
         "nt,nhij->thij", picks.astype(jnp.float32), d_scores, precision=lax.Precision.HIGHEST
     )
-    d_bias = lax.psum(local_tiles.astype(jnp.bfloat16), "seq").astype(jnp.float32)
+    d_bias = jnp.sum(lax.all_gather(local_tiles.astype(jnp.bfloat16), "seq"), axis=0).astype(
+        jnp.float32
+    )
     head_dgate = (
         head_dmix.astype(jnp.float32) * attended.astype(jnp.float32) * head_gate * (1.0 - head_gate)
     ).astype(jnp.bfloat16)

time: 315 us -> 290 us (0.921)
  waiting for transfers between devices: 134 us -> 105 us
  other arithmetic: 16.1 us -> 26.7 us
  local copies, waits for them, and re-layouts: 34.3 us -> 29.7 us
    psum x1 -> x0, waiting for transfers between devices: 76.6 us -> none  [shards(): lax.psum(local_tiles.astype(jnp.bfloat16), 'seq').astype(jnp.float32)]
    all_gather x0 -> x1, waiting for transfers between devices: none -> 44.8 us  [shards(): lax.all_gather(local_tiles.astype(jnp.bfloat16), 'seq')]
    all_to_all x1, waiting for transfers between devices: 9.37 us -> 0.01 us  [shards(): lax.all_to_all(values, 'head', split_axis=1, concat_axis=0, tiled=True)]
    reduce_sum x0 -> x1, other arithmetic: none -> 8.84 us  [shards(): jnp.sum(lax.all_gather(local_tiles.astype(jnp.bfloat16), 'seq'), axis=0)]
    all_to_all x1, waiting for transfers between devices: 0.01 us -> 5.6 us  [shards(): lax.all_to_all(d_mixed, 'head', split_axis=1, concat_axis=0, tiled=True)]
    all_to_all x1, waiting for transfers between devices: 0.01 us -> 4.98 us  [shards(): lax.all_to_all(d_keys, 'head', split_axis=0, concat_axis=1, tiled=True)]
    all_to_all x1, waiting for transfers between devices: 6.34 us -> 10.4 us  [shards(): lax.all_to_all(keys, 'head', split_axis=1, concat_axis=0, tiled=True)]
    all_to_all x1, starting transfers between devices: 5.28 us -> 8.59 us  [shards(): lax.all_to_all(keys, 'head', split_axis=1, concat_axis=0, tiled=True)]
  transfers between devices with their start and end apart: 14 -> 14, of which waited for: 8 -> 9; matrix products, arithmetic and copies ran while one was open for 25% -> 25% of each run, Pallas kernels for 0% -> 0%
where the time goes in v1:
time: 290 us; the launch traced here: 288 us
  waiting for transfers between devices  105 us (36%)
  starting transfers between devices  64 us (22%)
  matrix products  47.2 us (16%)
  local copies, waits for them, and re-layouts  29.7 us (10%)
  other arithmetic  26.7 us (9%)
  between operations  14.6 us (5%)
    all_gather x1, waiting for transfers between devices, shards(): lax.all_gather(local_tiles.astype(jnp.bfloat16), 'seq')  44.8 us
    sub x1, matrix products, attention_pass(): weights = jnp.where(mask, jnp.exp(scores - top), 0.0)  12.2 us
    all_to_all x1, waiting for transfers between devices, shards(): lax.all_to_all(queries, 'head', split_axis=1, concat_axis=0, tiled=True)  10.6 us
    all_to_all x1, waiting for transfers between devices, shards(): lax.all_to_all(keys, 'head', split_axis=1, concat_axis=0, tiled=True)  10.4 us
    ppermute x4, starting transfers between devices, passed_along(): return lax.ppermute(array, axis, pairs)  10.1 us
    all_to_all x1, waiting for transfers between devices, shards(): lax.all_to_all(gate_input, 'head', split_axis=1, concat_axis=0, tiled=True)  9.42 us
    all_to_all x1, waiting for transfers between devices, shards(): lax.all_to_all(d_values, 'head', split_axis=0, concat_axis=1, tiled=True)  9.08 us
    reduce_sum x1, other arithmetic, shards(): jnp.sum(lax.all_gather(local_tiles.astype(jnp.bfloat16), 'seq'), axis=0)  8.84 us
  transfers between devices with their start and end apart: 14, of which 9 were waited for; matrix products, arithmetic and copies ran while one was open for 25% of the time, Pallas kernels for 0%

profile of v1, /device:TPU:32, one launch (start us, length us, event | category | flops | bytes accessed | tf_op | source)
XLA Modules:
  0.0 287.7 jit_solution(6090530497361979526)
XLA Ops:
  7.2 1.2 convert_reduce_fusion
  8.4 1.2 fusion.30
  10.5 1.9 convolution_convert_fusion.5
  12.4 0.9 copy.96
  13.4 8.6 %all-to-all-start = ((bf16[256,16,48]{0,2,1:T(8,128)(2,1)}), bf16[256,16,48]{0,2,1:T(8,128)(2,1)S(1)}, u32[]{:S(2)}, u32[]{:S(2)}) async-start(bf16[256,16,48]{0,2,1:T(8,128)(2,1)} %bitcast), calls=%async_computation | async-start | bytes 786432 | tf_op jit(solution)/shard_map/all_to_all | solution.py:145
  22.5 0.9 copy.102
  23.4 10.4 %all-to-all-done = bf16[256,16,48]{0,2,1:T(8,128)(2,1)S(1)} async-done(((bf16[256,16,48]{0,2,1:T(8,128)(2,1)}), bf16[256,16,48]{0,2,1:T(8,128)(2,1)S(1)}, u32[]{:S(2)}, u32[]{:S(2)}) %all-to-all-start) | async-done | bytes 393248 | tf_op jit(solution)/shard_map/all_to_all | solution.py:145
  33.8 5.5 %all-to-all-start.1 = ((bf16[256,16,48]{0,2,1:T(8,128)(2,1)}), bf16[256,16,48]{0,2,1:T(8,128)(2,1)S(1)}, u32[]{:S(2)}, u32[]{:S(2)}) async-start(bf16[256,16,48]{0,2,1:T(8,128)(2,1)} %bitcast.6), calls=%async_computation.1 | async-start | bytes 786432 | tf_op jit(solution)/shard_map/all_to_all | solution.py:144
  39.9 0.9 copy.108
  40.8 10.6 %all-to-all-done.1 = bf16[256,16,48]{0,2,1:T(8,128)(2,1)S(1)} async-done(((bf16[256,16,48]{0,2,1:T(8,128)(2,1)}), bf16[256,16,48]{0,2,1:T(8,128)(2,1)S(1)}, u32[]{:S(2)}, u32[]{:S(2)}) %all-to-all-start.1) | async-done | bytes 393248 | tf_op jit(solution)/shard_map/all_to_all | solution.py:144
  51.5 5.4 %all-to-all-start.3 = ((bf16[256,16,48]{0,2,1:T(8,128)(2,1)}), bf16[256,16,48]{0,2,1:T(8,128)(2,1)S(1)}, u32[]{:S(2)}, u32[]{:S(2)}) async-start(bf16[256,16,48]{0,2,1:T(8,128)(2,1)} %bitcast.11), calls=%async_computation.3 | async-start | bytes 786432 | tf_op jit(solution)/shard_map/all_to_all | solution.py:147
  56.9 1.8 convolution_convert_fusion.3
  58.7 0.9 copy.107
  59.6 9.4 %all-to-all-done.3 = bf16[256,16,48]{0,2,1:T(8,128)(2,1)S(1)} async-done(((bf16[256,16,48]{0,2,1:T(8,128)(2,1)}), bf16[256,16,48]{0,2,1:T(8,128)(2,1)S(1)}, u32[]{:S(2)}, u32[]{:S(2)}) %all-to-all-start.3) | async-done | bytes 393248 | tf_op jit(solution)/shard_map/all_to_all | solution.py:147
  69.0 5.3 %all-to-all-start.2 = ((bf16[256,16,48]{0,2,1:T(8,128)(2,1)}), bf16[256,16,48]{0,2,1:T(8,128)(2,1)S(1)}, u32[]{:S(2)}, u32[]{:S(2)}) async-start(bf16[256,16,48]{0,2,1:T(8,128)(2,1)} %bitcast.10), calls=%async_computation.2 | async-start | bytes 786432 | tf_op jit(solution)/shard_map/all_to_all | solution.py:148
  75.3 1.8 convolution_convert_fusion.1
  77.1 0.9 copy.110
  78.0 1.5 convert_reduce_fusion.1
  79.6 1.3 fusion.43
  80.9 5.6 %all-to-all-done.2 = bf16[256,16,48]{0,2,1:T(8,128)(2,1)S(1)} async-done(((bf16[256,16,48]{0,2,1:T(8,128)(2,1)}), bf16[256,16,48]{0,2,1:T(8,128)(2,1)S(1)}, u32[]{:S(2)}, u32[]{:S(2)}) %all-to-all-start.2) | async-done | bytes 393248 | tf_op jit(solution)/shard_map/all_to_all | solution.py:148
  86.5 5.3 %all-to-all-start.4 = ((bf16[256,16,48]{0,2,1:T(8,128)(2,1)}), bf16[256,16,48]{0,2,1:T(8,128)(2,1)S(1)}, u32[]{:S(2)}, u32[]{:S(2)}) async-start(bf16[256,16,48]{0,2,1:T(8,128)(2,1)} %bitcast.171), calls=%async_computation.4 | async-start | bytes 786432 | tf_op jit(solution)/shard_map/all_to_all | solution.py:146
  91.8 1.4 eq.32
  93.2 1.3 convert_reduce_fusion.2
  94.5 4.0 %fusion.13 = f32[32,128,256]{2,0,1:T(8,128)} fusion(bf16[16,128,256]{2,1,0:T(8,128)(2,1)} %bitcast.184, s32[32]{0:T(128)} %param.20), kind=kOutput, calls=%fused_computation.29 | convolution fusion | flops 33554944 | bytes 5243008 | tf_op jit(solution)/shard_map/nt,thij->nhij/dot_general | solution.py:159
  98.6 4.1 %collective-permute-start = (bf16[128,48]{0,1:T(8,128)(2,1)S(1)}, bf16[128,48]{0,1:T(8,128)(2,1)}, u32[]{:S(2)}, u32[]{:S(2)}) collective-permute-start(bf16[128,48]{0,1:T(8,128)(2,1)S(1)} %slice.76), channel_id=1, source_target_pairs={{0,16},{16,32},{32,48},{48,64},{64,80},{80,96},{96,112},{112,128},... | collective-permute-start | bytes 36872 | tf_op jit(solution)/shard_map/ppermute | solution.py:14
  102.7 1.0 fusion.36
  103.8 0.9 reshape.258
  104.7 1.1 copy.99
  107.5 1.1 reshape.262
  108.6 1.3 copy.109
  109.9 0.9 reshape.273
  111.6 1.1 reshape.265
  114.4 3.5 %collective-permute-start.1 = (bf16[128,48]{0,1:T(8,128)(2,1)}, bf16[128,48]{0,1:T(8,128)(2,1)}, u32[]{:S(2)}, u32[]{:S(2)}) collective-permute-start(bf16[128,48]{0,1:T(8,128)(2,1)} %slice.78), channel_id=1, source_target_pairs={{0,16},{16,32},{32,48},{48,64},{64,80},{80,96},{96,112},{112,128},... | collective-permute-start | bytes 36872 | tf_op jit(solution)/shard_map/ppermute | solution.py:14
  117.9 12.2 %fusion.64 = (f32[32,128]{1,0:T(8,128)S(1)}, f32[32,128,256]{2,1,0:T(8,128)}) fusion(s32[32,256]{1,0:T(8,128)} %eq.32, s32[32,128]{1,0:T(8,128)} %bitcast.188, pred[32,256]{1,0:T(8,128)(4,1)} %fusion.43, f32[32,128,256]{2,0,1:T(8,128)} %fusion.13, bf16[32,128,48]{1,0,2:T(8,128)(2,1)S(1)} %reshape.262, bf16[32,128,1,48]{1,3,0,2:T(8,128)(2,1)S(1)} %copy.99, ...), kind=kOutput, calls=%fused_computation.106 | convolution fusion | flops 113508608 | bytes 9641984 | tf_op jit(solution)/shard_map/sub | solution.py:78
  130.1 4.1 %multiply_reduce_fusion = (f32[32,128]{1,0:T(8,128)S(1)}, f32[32,128,256]{2,1,0:T(8,128)S(1)}) fusion(f32[32,128,256]{2,1,0:T(8,128)} %get-tuple-element.9, f32[32,128]{1,0:T(8,128)S(1)} %get-tuple-element.8, bf16[32,128,1,48]{1,3,0,2:T(8,128)(2,1)S(1)} %copy-done.10, bf16[31,128,1,48]{1,3,0,2:T(8,128)(2,1)} %slice.79, bf16[1,128,1,48]{1,3,0,2:T(8,128)(2,1)} %bitcast.15, ...), kind=kOutput, calls=%fused_computation.6 | convolution fusion | flops 106164224 | bytes 9601024 | tf_op jit(solution)/shard_map/nihd,njhd->nhij/dot_general | solution.py:85
  134.2 1.4 subtract_multiply_fusion
  135.7 2.0 copy-done.1
  137.7 5.0 %fusion.4 = bf16[16,128,256]{2,0,1:T(8,128)(2,1)} fusion(f32[32,128,256]{2,1,0:T(8,128)S(1)} %subtract_multiply_fusion, s32[32]{0:T(128)S(1)} %copy-done.27), kind=kOutput, calls=%fused_computation.10 | convolution fusion | flops 201851392 | bytes 5243008 | tf_op jit(solution)/shard_map/nt,nhij->thij/dot_general | solution.py:174
  142.7 3.0 %fusion.16 = f32[32,48,256]{2,1,0:T(8,128)S(1)} fusion(bf16[32,128,48]{1,0,2:T(8,128)(2,1)S(1)} %copy-done.16, f32[32,128,256]{2,1,0:T(8,128)} %get-tuple-element.9, f32[32,128]{1,0:T(8,128)S(1)} %get-tuple-element.8), kind=kOutput, calls=%fused_computation.32 | convolution fusion | flops 102760448 | bytes 6176768 | tf_op jit(solution)/shard_map/nhij,nihd->njhd/dot_general | solution.py:98
  146.5 1.3 collective-permute-start.3
  147.8 1.5 fusion.9
  149.6 0.9 copy.117
  150.5 7.2 %all-to-all-start.5 = ((bf16[16,256,48]{1,2,0:T(8,128)(2,1)}), bf16[16,256,48]{1,2,0:T(8,128)(2,1)}, u32[]{:S(2)}, u32[]{:S(2)}) async-start(bf16[16,256,48]{1,2,0:T(8,128)(2,1)} %copy.117), calls=%async_computation.5 | async-start | bytes 786432 | tf_op jit(solution)/shard_map/all_to_all | solution.py:184
  157.7 1.3 slice_add_fusion
  159.0 2.8 convolution_multiply_fusion
  162.7 0.9 slice.81
  163.6 1.3 collective-permute-start.2
  166.4 3.3 %all-to-all-done.5 = bf16[16,256,48]{1,2,0:T(8,128)(2,1)} async-done(((bf16[16,256,48]{1,2,0:T(8,128)(2,1)}), bf16[16,256,48]{1,2,0:T(8,128)(2,1)}, u32[]{:S(2)}, u32[]{:S(2)}) %all-to-all-start.5) | async-done | bytes 393248 | tf_op jit(solution)/shard_map/all_to_all | solution.py:184
  169.7 5.9 %all-to-all-start.7 = ((bf16[16,256,48]{1,2,0:T(8,128)(2,1)}), bf16[16,256,48]{1,2,0:T(8,128)(2,1)}, u32[]{:S(2)}, u32[]{:S(2)}) async-start(bf16[16,256,48]{1,2,0:T(8,128)(2,1)} %bitcast.172), calls=%async_computation.7 | async-start | bytes 786432 | tf_op jit(solution)/shard_map/all_to_all | solution.py:186
  175.6 1.2 slice_add_fusion.1
  178.7 9.1 %all-to-all-done.7 = bf16[16,256,48]{1,2,0:T(8,128)(2,1)} async-done(((bf16[16,256,48]{1,2,0:T(8,128)(2,1)}), bf16[16,256,48]{1,2,0:T(8,128)(2,1)}, u32[]{:S(2)}, u32[]{:S(2)}) %all-to-all-start.7) | async-done | bytes 393248 | tf_op jit(solution)/shard_map/all_to_all | solution.py:186
  187.8 5.3 %all-to-all-start.6 = ((bf16[16,256,48]{1,2,0:T(8,128)(2,1)}), bf16[16,256,48]{1,2,0:T(8,128)(2,1)S(1)}, u32[]{:S(2)}, u32[]{:S(2)}) async-start(bf16[16,256,48]{1,2,0:T(8,128)(2,1)} %bitcast.159), calls=%async_computation.6 | async-start | bytes 786432 | tf_op jit(solution)/shard_map/all_to_all | solution.py:185
  193.1 3.3 %fusion.12 = f32[32,128,1,48]{1,3,0,2:T(8,128)S(1)} fusion(bf16[32,128,1,48]{1,3,0,2:T(8,128)(2,1)S(1)} %copy-done.11, bf16[31,128,1,48]{1,3,0,2:T(8,128)(2,1)S(1)} %copy-done.18, bf16[1,128,1,48]{1,3,0,2:T(8,128)(2,1)} %bitcast.15, f32[32,128,256]{2,1,0:T(8,128)} %get-tuple-element.9, f32[32,128]{1,0:T(8,128)S(1)} %get-tuple-element.8), kind=kOutput, calls=%fused_computation.27 | convolution fusion | flops 105512960 | bytes 5783552 | tf_op jit(solution)/shard_map/nhij,njhd->nihd/dot_general | solution.py:81
  196.7 1.1 reshape.270
  197.8 2.5 fusion.35
  200.3 5.0 %all-to-all-done.6 = bf16[16,256,48]{1,2,0:T(8,128)(2,1)S(1)} async-done(((bf16[16,256,48]{1,2,0:T(8,128)(2,1)}), bf16[16,256,48]{1,2,0:T(8,128)(2,1)S(1)}, u32[]{:S(2)}, u32[]{:S(2)}) %all-to-all-start.6) | async-done | bytes 393248 | tf_op jit(solution)/shard_map/all_to_all | solution.py:185
  205.3 5.3 %all-to-all-start.8 = ((bf16[16,256,48]{1,2,0:T(8,128)(2,1)}), bf16[16,256,48]{1,2,0:T(8,128)(2,1)S(1)}, u32[]{:S(2)}, u32[]{:S(2)}) async-start(bf16[16,256,48]{1,2,0:T(8,128)(2,1)} %fusion.35), calls=%async_computation.8 | async-start | bytes 786432 | tf_op jit(solution)/shard_map/all_to_all | solution.py:187
  210.5 2.0 fusion.67
  213.8 1.5 convolution_add_fusion.1
  215.3 7.3 %all-to-all-done.8 = bf16[16,256,48]{1,2,0:T(8,128)(2,1)S(1)} async-done(((bf16[16,256,48]{1,2,0:T(8,128)(2,1)}), bf16[16,256,48]{1,2,0:T(8,128)(2,1)S(1)}, u32[]{:S(2)}, u32[]{:S(2)}) %all-to-all-start.8) | async-done | bytes 393248 | tf_op jit(solution)/shard_map/all_to_all | solution.py:187
  223.4 1.0 fusion.29
  224.4 44.8 %all-gather.3.cloned.1.call-done = bf16[256,128,256]{2,0,1:T(8,128)(2,1)} async-done(((bf16[16,128,256]{2,0,1:T(8,128)(2,1)}), bf16[256,128,256]{2,0,1:T(8,128)(2,1)}) %all-gather.3.cloned.1.call-update) | async-done | bytes 16777232 | tf_op jit(solution)/shard_map/all_gather | solution.py:177
  269.1 8.8 %reduce.8 = bf16[16,128,256]{2,0,1:T(8,128)(2,1)S(1)} reduce(bf16[16,16,128,256]{3,1,0,2:T(8,128)(2,1)} %bitcast.162, bf16[]{:T(256)} %constant.39.clone.1), dimensions={0}, to_apply=%region_10.11 | reduce | flops 7864320 | bytes 17825794 | tf_op jit(solution)/shard_map/reduce_sum | solution.py:177
  278.3 2.5 copy.131
  (108 shorter events, 15.0 us)
Async XLA Ops:
  7.2 32.2 %copy-start = (bf16[768,768]{1,0:T(8,128)(2,1)S(1)}, bf16[768,768]{1,0:T(8,128)(2,1)}, u32[]{:S(2)}) copy-start(bf16[768,768]{1,0:T(8,128)(2,1)} %param.16) | copy-start | bytes 3538948
  8.4 66.9 %copy-start.19 = (f32[256]{0:T(256)}, f32[256]{0:T(256)S(1)}, u32[]{:S(2)}) copy-start(f32[256]{0:T(256)S(1)} %broadcast_multiply_fusion.2) | copy-start | bytes 3076
  9.7 12.3 %copy-start.3 = (bf16[256,768]{1,0:T(8,128)(2,1)S(1)}, bf16[256,768]{1,0:T(8,128)(2,1)}, u32[]{:S(2)}) copy-start(bf16[256,768]{1,0:T(8,128)(2,1)} %param.11) | copy-start | bytes 1179652
  9.7 12.3 %copy-start.15 = (bf16[768,768]{1,0:T(8,128)(2,1)S(1)}, bf16[768,768]{1,0:T(8,128)(2,1)}, u32[]{:S(2)}) copy-start(bf16[768,768]{1,0:T(8,128)(2,1)} %param.13) | copy-start | bytes 3538948
  9.7 65.6 %copy-start.23 = (f32[256]{0:T(256)}, f32[256]{0:T(256)S(1)}, u32[]{:S(2)}) copy-start(f32[256]{0:T(256)S(1)} %add_rsqrt_fusion) | copy-start | bytes 3076
  10.5 64.8 %copy-start.21 = (f32[768]{0:T(1024)}, f32[768]{0:T(1024)S(1)}, u32[]{:S(2)}) copy-start(f32[768]{0:T(1024)S(1)} %convert_element_type.153) | copy-start | bytes 9220
  13.4 20.5 %all-to-all-start = ((bf16[256,16,48]{0,2,1:T(8,128)(2,1)}), bf16[256,16,48]{0,2,1:T(8,128)(2,1)S(1)}, u32[]{:S(2)}, u32[]{:S(2)}) async-start(bf16[256,16,48]{0,2,1:T(8,128)(2,1)} %bitcast), calls=%async_computation | async-start | bytes 786432 | tf_op jit(solution)/shard_map/all_to_all | solution.py:145
  33.8 17.6 %all-to-all-start.1 = ((bf16[256,16,48]{0,2,1:T(8,128)(2,1)}), bf16[256,16,48]{0,2,1:T(8,128)(2,1)S(1)}, u32[]{:S(2)}, u32[]{:S(2)}) async-start(bf16[256,16,48]{0,2,1:T(8,128)(2,1)} %bitcast.6), calls=%async_computation.1 | async-start | bytes 786432 | tf_op jit(solution)/shard_map/all_to_all | solution.py:144
  39.4 17.5 %copy-start.17 = (bf16[256,768]{1,0:T(8,128)(2,1)S(1)}, bf16[256,768]{1,0:T(8,128)(2,1)}, u32[]{:S(2)}) copy-start(bf16[256,768]{1,0:T(8,128)(2,1)} %param.21) | copy-start | bytes 1179652
  51.5 23.6 %copy-start.28 = (s32[16]{0:T(128)S(1)}, s32[16]{0:T(128)}, u32[]{:S(2)}) copy-start(s32[16]{0:T(128)} %param.19) | copy-start | bytes 196
  51.5 17.6 %all-to-all-start.3 = ((bf16[256,16,48]{0,2,1:T(8,128)(2,1)}), bf16[256,16,48]{0,2,1:T(8,128)(2,1)S(1)}, u32[]{:S(2)}, u32[]{:S(2)}) async-start(bf16[256,16,48]{0,2,1:T(8,128)(2,1)} %bitcast.11), calls=%async_computation.3 | async-start | bytes 786432 | tf_op jit(solution)/shard_map/all_to_all | solution.py:147
  59.6 15.5 %copy-start.26 = (s32[32]{0:T(128)}, s32[32]{0:T(128)S(1)}, u32[]{:S(2)}) copy-start(s32[32]{0:T(128)S(1)} %add_add_fusion) | copy-start | bytes 388
  69.0 17.4 %all-to-all-start.2 = ((bf16[256,16,48]{0,2,1:T(8,128)(2,1)}), bf16[256,16,48]{0,2,1:T(8,128)(2,1)S(1)}, u32[]{:S(2)}, u32[]{:S(2)}) async-start(bf16[256,16,48]{0,2,1:T(8,128)(2,1)} %bitcast.10), calls=%async_computation.2 | async-start | bytes 786432 | tf_op jit(solution)/shard_map/all_to_all | solution.py:148
  75.3 16.5 %copy-start.25 = (s32[16]{0:T(128)}, s32[16]{0:T(128)S(1)}, u32[]{:S(2)}) copy-start(s32[16]{0:T(128)S(1)} %reduce.9) | copy-start | bytes 196
  86.5 16.2 %copy-start.5 = (bf16[256,16,48]{0,2,1:T(8,128)(2,1)}, bf16[256,16,48]{0,2,1:T(8,128)(2,1)S(1)}, u32[]{:S(2)}) copy-start(bf16[256,16,48]{0,2,1:T(8,128)(2,1)S(1)} %all-to-all-done.2) | copy-start | bytes 1179652
  86.5 24.3 %all-to-all-start.4 = ((bf16[256,16,48]{0,2,1:T(8,128)(2,1)}), bf16[256,16,48]{0,2,1:T(8,128)(2,1)S(1)}, u32[]{:S(2)}, u32[]{:S(2)}) async-start(bf16[256,16,48]{0,2,1:T(8,128)(2,1)} %bitcast.171), calls=%async_computation.4 | async-start | bytes 786432 | tf_op jit(solution)/shard_map/all_to_all | solution.py:146
  91.7 177.4 %all-gather.3.cloned.1.call-start = ((), (), s32[]{:S(2)}) async-start(), calls=%async_computation.9 | async-start | bytes 17825792 | tf_op jit(solution)/shard_map/all_gather | solution.py:177
  98.6 19.3 %collective-permute-start = (bf16[128,48]{0,1:T(8,128)(2,1)S(1)}, bf16[128,48]{0,1:T(8,128)(2,1)}, u32[]{:S(2)}, u32[]{:S(2)}) collective-permute-start(bf16[128,48]{0,1:T(8,128)(2,1)S(1)} %slice.76), channel_id=1, source_target_pairs={{0,16},{16,32},{32,48},{48,64},{64,80},{80,96},{96,112},{112,128},... | collective-permute-start | bytes 36872 | tf_op jit(solution)/shard_map/ppermute | solution.py:14
  108.6 9.3 %copy-start.7 = (bf16[32,128,48]{1,0,2:T(8,128)(2,1)}, bf16[32,128,48]{1,0,2:T(8,128)(2,1)S(1)}, u32[]{:S(2)}) copy-start(bf16[32,128,48]{1,0,2:T(8,128)(2,1)S(1)} %reshape.262) | copy-start | bytes 1179652
  112.9 0.9 copy-start.9
  114.4 15.7 %collective-permute-start.1 = (bf16[128,48]{0,1:T(8,128)(2,1)}, bf16[128,48]{0,1:T(8,128)(2,1)}, u32[]{:S(2)}, u32[]{:S(2)}) collective-permute-start(bf16[128,48]{0,1:T(8,128)(2,1)} %slice.78), channel_id=1, source_target_pairs={{0,16},{16,32},{32,48},{48,64},{64,80},{80,96},{96,112},{112,128},... | collective-permute-start | bytes 36872 | tf_op jit(solution)/shard_map/ppermute | solution.py:14
  117.9 12.2 %copy-start.10 = (bf16[32,128,1,48]{1,3,0,2:T(8,128)(2,1)S(1)}, bf16[32,128,1,48]{1,3,0,2:T(8,128)(2,1)}, u32[]{:S(2)}) copy-start(bf16[32,128,1,48]{1,3,0,2:T(8,128)(2,1)} %copy-done.9) | copy-start | bytes 1179652
  117.9 12.2 %copy-start.16 = (bf16[32,128,48]{1,0,2:T(8,128)(2,1)S(1)}, bf16[32,128,48]{1,0,2:T(8,128)(2,1)}, u32[]{:S(2)}) copy-start(bf16[32,128,48]{1,0,2:T(8,128)(2,1)} %reshape.273) | copy-start | bytes 1179652
  130.1 4.1 %copy-start.4 = (f32[32,128,256]{2,1,0:T(8,128)S(1)}, f32[32,128,256]{2,1,0:T(8,128)}, u32[]{:S(2)}) copy-start(f32[32,128,256]{2,1,0:T(8,128)} %get-tuple-element.9) | copy-start | bytes 12582916
  134.2 3.4 %copy-start.27 = (s32[32]{0:T(128)S(1)}, s32[32]{0:T(128)}, u32[]{:S(2)}) copy-start(s32[32]{0:T(128)} %param.20) | copy-start | bytes 388
  135.7 2.0 copy-start.1
  142.7 5.1 %copy-start.2 = (f32[32,128,256]{2,1,0:T(8,128)S(1)}, f32[32,128,256]{2,1,0:T(8,128)}, u32[]{:S(2)}) copy-start(f32[32,128,256]{2,1,0:T(8,128)} %copy-done.1) | copy-start | bytes 12582916
  142.7 5.1 %copy-start.12 = (bf16[31,128,1,48]{1,3,0,2:T(8,128)(2,1)S(1)}, bf16[31,128,1,48]{1,3,0,2:T(8,128)(2,1)}, u32[]{:S(2)}) copy-start(bf16[31,128,1,48]{1,3,0,2:T(8,128)(2,1)} %slice.77) | copy-start | bytes 1142788
  145.7 3.6 %copy-start.8 = (f32[32,48,256]{2,1,0:T(8,128)}, f32[32,48,256]{2,1,0:T(8,128)S(1)}, u32[]{:S(2)}) copy-start(f32[32,48,256]{2,1,0:T(8,128)S(1)} %fusion.16) | copy-start | bytes 4718596
  146.5 18.4 %collective-permute-start.3 = (bf16[128,48]{0,1:T(8,128)(2,1)}, bf16[128,48]{0,1:T(8,128)(2,1)}, u32[]{:S(2)}, u32[]{:S(2)}) collective-permute-start(bf16[128,48]{0,1:T(8,128)(2,1)} %fusion.49), channel_id=1, source_target_pairs={{16,0},{32,16},{48,32},{64,48},{80,64},{96,80},{112,96},{128,112},... | collective-permute-start | bytes 36872 | tf_op jit(solution)/shard_map/ppermute | solution.py:14
  150.5 19.2 %all-to-all-start.5 = ((bf16[16,256,48]{1,2,0:T(8,128)(2,1)}), bf16[16,256,48]{1,2,0:T(8,128)(2,1)}, u32[]{:S(2)}, u32[]{:S(2)}) async-start(bf16[16,256,48]{1,2,0:T(8,128)(2,1)} %copy.117), calls=%async_computation.5 | async-start | bytes 786432 | tf_op jit(solution)/shard_map/all_to_all | solution.py:184
  163.6 13.6 %collective-permute-start.2 = (bf16[128,48]{0,1:T(8,128)(2,1)}, bf16[128,48]{0,1:T(8,128)(2,1)}, u32[]{:S(2)}, u32[]{:S(2)}) collective-permute-start(bf16[128,48]{0,1:T(8,128)(2,1)} %fusion.48), channel_id=1, source_target_pairs={{16,0},{32,16},{48,32},{64,48},{80,64},{96,80},{112,96},{128,112},... | collective-permute-start | bytes 36872 | tf_op jit(solution)/shard_map/ppermute | solution.py:14
  169.7 18.1 %all-to-all-start.7 = ((bf16[16,256,48]{1,2,0:T(8,128)(2,1)}), bf16[16,256,48]{1,2,0:T(8,128)(2,1)}, u32[]{:S(2)}, u32[]{:S(2)}) async-start(bf16[16,256,48]{1,2,0:T(8,128)(2,1)} %bitcast.172), calls=%async_computation.7 | async-start | bytes 786432 | tf_op jit(solution)/shard_map/all_to_all | solution.py:186
  176.9 16.2 %copy-start.11 = (bf16[32,128,1,48]{1,3,0,2:T(8,128)(2,1)S(1)}, bf16[32,128,1,48]{1,3,0,2:T(8,128)(2,1)}, u32[]{:S(2)}) copy-start(bf16[32,128,1,48]{1,3,0,2:T(8,128)(2,1)} %copy-done.9) | copy-start | bytes 1179652
  176.9 16.2 %copy-start.18 = (bf16[31,128,1,48]{1,3,0,2:T(8,128)(2,1)S(1)}, bf16[31,128,1,48]{1,3,0,2:T(8,128)(2,1)}, u32[]{:S(2)}) copy-start(bf16[31,128,1,48]{1,3,0,2:T(8,128)(2,1)} %slice.79) | copy-start | bytes 1142788
  187.8 17.5 %all-to-all-start.6 = ((bf16[16,256,48]{1,2,0:T(8,128)(2,1)}), bf16[16,256,48]{1,2,0:T(8,128)(2,1)S(1)}, u32[]{:S(2)}, u32[]{:S(2)}) async-start(bf16[16,256,48]{1,2,0:T(8,128)(2,1)} %bitcast.159), calls=%async_computation.6 | async-start | bytes 786432 | tf_op jit(solution)/shard_map/all_to_all | solution.py:185
  196.5 1.4 copy-start.6
  205.3 17.4 %all-to-all-start.8 = ((bf16[16,256,48]{1,2,0:T(8,128)(2,1)}), bf16[16,256,48]{1,2,0:T(8,128)(2,1)S(1)}, u32[]{:S(2)}, u32[]{:S(2)}) async-start(bf16[16,256,48]{1,2,0:T(8,128)(2,1)} %fusion.35), calls=%async_computation.8 | async-start | bytes 786432 | tf_op jit(solution)/shard_map/all_to_all | solution.py:187
  210.5 2.0 copy-start.13
  212.5 1.3 copy-start.14
  213.1 9.5 %copy-start.20 = (f32[256]{0:T(256)S(1)}, f32[256]{0:T(256)}, u32[]{:S(2)}) copy-start(f32[256]{0:T(256)} %copy-done.19) | copy-start | bytes 3076
  213.1 9.5 %copy-start.22 = (f32[768]{0:T(1024)S(1)}, f32[768]{0:T(1024)}, u32[]{:S(2)}) copy-start(f32[768]{0:T(1024)} %copy-done.21) | copy-start | bytes 9220
  213.1 9.5 %copy-start.24 = (f32[256]{0:T(256)S(1)}, f32[256]{0:T(256)}, u32[]{:S(2)}) copy-start(f32[256]{0:T(256)} %copy-done.23) | copy-start | bytes 3076
Sparse Core Ops, SparseCore 0:
  142.8 126.2 all-gather.2
